TPU v7x, 512 devices: a whole 4x4x16 slice. The times are simulated.
512 devices in a mesh: frames: 32 (over y, x, core), atoms: 16 (over z).
Axes of the slice: x: 4, y: 4, z: 16, core: 2. Of those that a mesh axis runs over, the one named last changes fastest.
Arguments:
- frames: float32 [2048, 3, 6144], P('frames', None, 'atoms'), may hold values from -45 to 45, as said below
- reference_structure: float32 [3, 6144], P(None, 'atoms'), may hold values from -15 to 15
Outputs:
- covariance: float32 [3, 6144, 3, 6144], P(None, 'frames', None, 'atoms')
- mean_structure: float32 [3, 6144], P(None, 'atoms')
Inputs may be any that keep to these rules, and one draw needn't show every extreme that they name: `frames`: every frame, once centered, has a cross-covariance with the centered reference_structure of positive determinant whose singular values lie within a factor of 20 of one another.
All inputs are finite; a program needn't handle non-finite values.
Results may differ from a plain program's by a relative error of at most 0.0003.
Values may be sent and summed in bfloat16 or wider, within the bound.
A program may use at most 64 MiB of HBM per device.

v0:
```python
import jax
import jax.numpy as jnp
from jax import lax
from jax.sharding import Mesh
from jax.sharding import PartitionSpec as P

ATOMS = 6144
ITERS = 2
POLAR = 8
FRAMES = ("frames_0", "frames_1", "frames_2")


def copy_for_each(array, axis):
    copies = jnp.broadcast_to(array, (lax.axis_size(axis), *array.shape))
    return lax.all_to_all(copies, axis, split_axis=0, concat_axis=0, tiled=True)


def over_copies(array, axis):
    everything = copy_for_each(array, axis)
    return jnp.sum(everything, axis=0)


def in_one(arrays, axis):
    vector, at, finished = (jnp.concatenate([a.reshape(-1) for a in arrays]), 0, [])
    total = over_copies(vector, axis)
    for a in arrays:
        finished.append(total[at : at + a.size].reshape(a.shape))
        at += a.size
    return tuple(finished)


def in_blocks(array, dim, devices):
    lengths = array.shape
    blocks = array.reshape(*lengths[:dim], devices, lengths[dim] // devices, *lengths[dim + 1 :])
    return jnp.moveaxis(blocks, dim, 0)


def laid_out(blocks, dim):
    blocks = jnp.moveaxis(blocks, 0, dim)
    lengths = blocks.shape
    return blocks.reshape(*lengths[:dim], lengths[dim] * lengths[dim + 1], *lengths[dim + 2 :])


def exchange_in_order(blocks, axes, turns):
    lengths = [lax.axis_size(a) for a in axes]
    blocks = blocks.reshape(*lengths, *blocks.shape[1:])
    for k in turns:
        blocks = lax.all_to_all(blocks, axes[k], split_axis=k, concat_axis=k, tiled=True)
    return blocks.reshape(-1, *blocks.shape[len(axes) :])


def core_and_chips(array, groups, turns, split_dim, concat_dim):
    devices = lax.axis_size(groups[0]) * lax.axis_size(groups[1])
    blocks = in_blocks(array, split_dim, devices)
    return laid_out(exchange_in_order(blocks, groups, turns), concat_dim)


def polar_factor(cross):
    factor = jnp.sqrt(3.0 / jnp.sum(cross * cross, axis=(0, 1)))
    matrix = cross * factor[None, None, :]
    for turn in range(POLAR):
        entries = [[matrix[i, j] for j in range(3)] for i in range(3)]
        cofactor = [
            [
                entries[(i + 1) % 3][(j + 1) % 3] * entries[(i + 2) % 3][(j + 2) % 3]
                - entries[(i + 1) % 3][(j + 2) % 3] * entries[(i + 2) % 3][(j + 1) % 3]
                for j in range(3)
            ]
            for i in range(3)
        ]
        determinant = (
            entries[0][0] * cofactor[0][0]
            + entries[0][1] * cofactor[0][1]
            + entries[0][2] * cofactor[0][2]
        )
        inverse = jnp.stack([jnp.stack(cofactor[i]) for i in range(3)]) / determinant[None, None, :]
        matrix = 0.5 * (matrix + inverse)
    return matrix


def contract_frames(left_rows, right_rows):
    return lax.dot_general(
        left_rows, right_rows, (((0,), (0,)), ((), ())), preferred_element_type=jnp.float32
    )


def body(frames, reference_structure):
    highest = lax.Precision.HIGHEST
    mean_now = reference_structure
    count_all = frames.shape[0] * lax.axis_size(FRAMES)
    for iteration in range(ITERS):
        sum_coords, sum_cross, sum_mean = in_one(
            (
                jnp.sum(frames, axis=2),
                jnp.einsum("fca,da->cdf", frames, mean_now, precision=highest),
                jnp.sum(mean_now, axis=1),
            ),
            "atoms",
        )
        centroid = sum_coords / ATOMS
        cross = sum_cross - centroid.T[:, None, :] * sum_mean[None, :, None]
        shifted = frames - centroid[:, :, None]
        rotation = polar_factor(cross)
        aligned = jnp.einsum("cdf,fca->fda", rotation, shifted, precision=highest)
        mean_now = over_copies(jnp.sum(aligned, axis=0), FRAMES) / count_all
    deviation = (aligned - mean_now[None]).astype(jnp.bfloat16)
    column_atoms = frames.shape[2]
    row_count = column_atoms * lax.axis_size("atoms") // lax.axis_size(FRAMES)
    own_rows = lax.all_gather(deviation, "atoms", axis=2, tiled=True)
    row_panel = core_and_chips(own_rows, (("frames_0", "frames_1"), "frames_2"), (1, 0), 2, 0)
    row_flat = row_panel.reshape(row_panel.shape[0], 3 * row_count)
    piece = lax.all_gather(deviation, FRAMES, axis=0, tiled=True)
    product = contract_frames(row_flat, piece.reshape(piece.shape[0], 3 * column_atoms))
    covariance = (product / count_all).reshape(3, row_count, 3, column_atoms)
    return (covariance, mean_now)


def solution(mesh):
    finer = Mesh(
        mesh.devices.reshape(4, 4, 2, mesh.shape["atoms"]),
        ("frames_0", "frames_1", "frames_2", "atoms"),
    )
    return jax.shard_map(
        body,
        mesh=finer,
        in_specs=(P(FRAMES, None, "atoms"), P(None, "atoms")),
        out_specs=(P(None, FRAMES, None, "atoms"), P(None, "atoms")),
        check_vma=False,
    )
```

profile of v0, /device:TPU:2, one launch (start us, length us, event | category | flops | bytes accessed | tf_op | source)
XLA Modules:
  0.0 281.3 jit_solution(8115866642797572257)
XLA Ops:
  7.2 0.8 reduce_sum.99
  8.1 1.1 reduce_sum.98
  9.1 1.4 convolution_bitcast_fusion.2
  10.6 0.1 reshape.5854
  10.7 0.1 copy.45
  10.8 0.1 reshape.5853
  11.1 27.7 %all_to_all.32 = f32[16,1,771]{2,1,0:T(1,128)S(1)} all-to-all(f32[16,1,771]{2,1,0:T(1,128)S(1)} %broadcast_in_dim.8), channel_id=1, replica_groups=mesh['frames_0'=4,'frames_1'=4,'frames_2'=2,'atoms'=16] {'atoms'}, dimensions={0} | all-to-all | bytes 98688 | tf_op jit(solution)/shard_map/all_to_all | solution.py:15
  39.0 0.1 div.197
  39.3 0.1 multiply_reduce_fusion.1
  39.9 0.1 fusion.9
  40.0 0.1 fusion.10
  40.2 0.1 fusion.11
  40.4 0.1 fusion.12
  40.5 0.1 fusion.13
  40.7 1.3 convolution_bitcast_fusion.1
  42.1 14.4 %all_to_all.33 = f32[32,3,384]{2,1,0:T(4,128)S(1)} all-to-all(f32[32,3,384]{2,1,0:T(4,128)S(1)} %broadcast_in_dim.9), channel_id=1, replica_groups=mesh['frames_0'=4,'frames_1'=4,'frames_2'=2,'atoms'=16] {'frames_0','fra..., dimensions={0} | all-to-all | bytes 294912 | tf_op jit(solution)/shard_map/all_to_all | solution.py:15
  56.6 0.1 multiply_reduce_fusion.2
  56.7 1.4 convolution_bitcast_fusion
  58.1 0.1 reshape.5856
  58.4 15.9 %all_to_all.34 = f32[16,1,771]{2,1,0:T(1,128)S(1)} all-to-all(f32[16,1,771]{2,1,0:T(1,128)S(1)} %broadcast_in_dim.10), channel_id=1, replica_groups=mesh['frames_0'=4,'frames_1'=4,'frames_2'=2,'atoms'=16] {'atoms'}, dimensions={0} | all-to-all | bytes 98688 | tf_op jit(solution)/shard_map/all_to_all | solution.py:15
  74.5 0.1 div.225
  74.8 0.1 multiply_reduce_fusion
  75.4 0.1 fusion.16
  75.5 0.1 fusion.17
  75.7 0.1 fusion.18
  75.9 0.1 fusion.19
  76.0 0.1 fusion.20
  76.2 0.1 fusion.21
  76.4 0.1 copy.53
  76.5 0.1 broadcast_subtract_fusion
  76.6 1.1 fusion.33
  77.7 11.5 %all_to_all.35 = f32[32,3,384]{2,1,0:T(4,128)S(1)} all-to-all(f32[32,3,384]{2,1,0:T(4,128)S(1)} %broadcast_in_dim.11), channel_id=1, replica_groups=mesh['frames_0'=4,'frames_1'=4,'frames_2'=2,'atoms'=16] {'frames_0','fra..., dimensions={0} | all-to-all | bytes 294912 | tf_op jit(solution)/shard_map/all_to_all | solution.py:15
  89.3 0.7 subtract_convert_fusion
  90.1 1.6 copy.60
  91.7 75.2 %all-gather.3.cloned.1.call-done = bf16[64,3,6144]{2,1,0:T(4,128)(2,1)} async-done(((bf16[64,3,384]{2,1,0:T(4,128)(2,1)}), bf16[64,3,6144]{2,1,0:T(4,128)(2,1)}) %all-gather.3.cloned.1.call-update) | async-done | bytes 2359312 | tf_op jit(solution)/shard_map/all_gather | solution.py:109
  166.9 3.6 %copy.56 = bf16[64,3,6144]{2,0,1:T(8,128)(2,1)S(1)} copy(bf16[64,3,6144]{2,1,0:T(4,128)(2,1)} %all-gather.3.cloned.1.call-done) | data formatting | bytes 4718592 | tf_op jit(solution)/shard_map/all_gather | solution.py:109
  170.5 4.6 %reshape.5858 = bf16[64,3,32,192]{3,2,0,1:T(8,128)(2,1)} reshape(bf16[64,3,6144]{2,0,1:T(8,128)(2,1)S(1)} %copy.56) | data formatting | bytes 4718592 | tf_op jit(solution)/shard_map/reshape | solution.py:34
  175.1 4.3 %reshape.5859 = bf16[16,2,64,3,192]{4,1,0,2,3:T(2,128)(2,1)S(1)} reshape(bf16[32,64,3,192]{3,0,1,2:T(8,128)(2,1)} %bitcast.395) | data formatting | bytes 4718592 | tf_op jit(solution)/shard_map/reshape | solution.py:46
  179.4 1.8 copy.57
  181.2 6.3 %all_to_all.36 = bf16[16,2,64,3,192]{4,2,3,0,1:T(8,128)(2,1)S(1)} all-to-all(bf16[16,2,64,3,192]{4,2,3,0,1:T(8,128)(2,1)S(1)} %copy.57), channel_id=1, replica_groups=mesh['frames_0'=4,'frames_1'=4,'frames_2'=2,'atoms'=16] {'frames_2'}, dimensions={1} | all-to-all | bytes 4718592 | tf_op jit(solution)/shard_map/all_to_all | solution.py:48
  187.4 0.4 copy.58
  187.8 53.9 %all_to_all.37 = bf16[16,2,64,3,192]{4,2,3,1,0:T(8,128)(2,1)S(1)} all-to-all(bf16[16,2,64,3,192]{4,2,3,1,0:T(8,128)(2,1)S(1)} %copy.58), channel_id=1, replica_groups=mesh['frames_0'=4,'frames_1'=4,'frames_2'=2,'atoms'=16] {'frames_0','fra..., dimensions={0} | all-to-all | bytes 4718592 | tf_op jit(solution)/shard_map/all_to_all | solution.py:48
  241.7 5.0 %copy.59 = bf16[16,2,64,3,192]{4,3,2,1,0:T(4,128)(2,1)} copy(bf16[16,2,64,3,192]{4,2,3,1,0:T(8,128)(2,1)S(1)} %all_to_all.37) | data formatting | bytes 4718592 | tf_op jit(solution)/shard_map/all_to_all | solution.py:48
  246.8 8.0 %reshape_reshape_reshape.3 = bf16[2048,576]{1,0:T(8,128)(2,1)S(1)} reshape(bf16[16,2,64,3,192]{4,3,2,1,0:T(4,128)(2,1)} %copy.59) | data formatting | bytes 4718592 | tf_op jit(solution)/shard_map/reshape;reshape;reshape | solution.py:111
  254.8 6.7 %copy.61 = bf16[2048,3,384]{0,2,1:T(8,128)(2,1)} copy(bf16[2048,3,384]{2,0,1:T(8,128)(2,1)} %all-gather.5.cloned.1.call-done) | data formatting | bytes 9437184 | tf_op jit(solution)/shard_map/all_gather | solution.py:112
  261.6 7.4 %convolution_multiply_fusion = f32[576,1152]{1,0:T(8,128)} fusion(bf16[2048,576]{1,0:T(8,128)(2,1)S(1)} %reshape_reshape_reshape.3, bf16[2048,1152]{0,1:T(8,128)(2,1)} %bitcast.396), kind=kOutput, calls=%fused_computation | convolution fusion | flops 2718572544 | bytes 9732096 | tf_op jit(solution)/shard_map/dot_general | solution.py:82
  269.0 3.7 %reshape.5861 = f32[3,192,3,384]{3,2,1,0:T(4,128)S(1)} reshape(f32[576,1152]{1,0:T(8,128)} %convolution_multiply_fusion) | data formatting | bytes 5308416 | tf_op jit(solution)/shard_map/reshape | solution.py:114
  272.7 1.7 copy.62
  (119 shorter events, 2.6 us)
Async XLA Ops:
  7.2 69.3 %copy-start = (f32[64,3,384]{2,0,1:T(8,128)S(1)}, f32[64,3,384]{2,0,1:T(8,128)}, u32[]{:S(2)}) copy-start(f32[64,3,384]{2,0,1:T(8,128)} %param.2) | copy-start | bytes 884740
  7.2 159.8 %all-gather.3.cloned.1.call-start = ((), (), s32[]{:S(2)}) async-start(), calls=%async_computation.6 | async-start | bytes 3342336 | tf_op jit(solution)/shard_map/all_gather | solution.py:109
  89.3 81.3 %copy-start.1 = (f32[3,384]{1,0:T(4,128)}, f32[3,384]{1,0:T(4,128)S(1)}, u32[]{:S(2)}) copy-start(f32[3,384]{1,0:T(4,128)S(1)} %broadcast_multiply_fusion) | copy-start | bytes 13828
  90.1 164.8 %all-gather.5.cloned.1.call-start = ((), (), s32[]{:S(2)}) async-start(), calls=%async_computation.7 | async-start | bytes 4866048 | tf_op jit(solution)/shard_map/all_gather | solution.py:112
Sparse Core Ops, SparseCore 0:
  90.2 76.7 all-gather.2
  170.1 73.4 all-gather.4
where the time goes:
time: 282 us; the launch traced here: 281 us
  blocking collectives  130 us (46%)
  waiting for transfers between devices  75.2 us (27%)
  local copies, waits for them, and re-layouts  43.1 us (15%)
  between operations  14.7 us (5%)
  matrix products  12.7 us (5%)
  other arithmetic  5.79 us (2%)
    all_gather x1, waiting for transfers between devices, body(): own_rows = lax.all_gather(deviation, 'atoms', axis=2, tiled=True)  75.2 us
    all_to_all x4, blocking collectives, copy_for_each(): return lax.all_to_all(copies, axis, split_axis=0, concat_axis=0, tiled=True)  69.5 us
    all_to_all x2, blocking collectives, exchange_in_order(): lax.all_to_all(blocks, axes[k], split_axis=k, concat_axis=k, tiled=True)  60.2 us
    another operation x1, local copies, waits for them, and re-layouts, body(): row_flat = row_panel.reshape(row_panel.shape[0], 3 * row_count)  8.03 us
    dot_general x1, matrix products, contract_frames(): lax.dot_general(left_rows, right_rows, (((0,), (0,)), ((), ())), preferre...  7.42 us
    all_gather x1, local copies, waits for them, and re-layouts, body(): piece = lax.all_gather(deviation, FRAMES, axis=0, tiled=True)  6.75 us
    reshape x2, local copies, waits for them, and re-layouts, exchange_in_order(): blocks = blocks.reshape(*lengths, *blocks.shape[1:])  6.04 us
  transfers between devices with their start and end apart: 2, of which 1 were waited for; matrix products, arithmetic and copies ran while one was open for 10% of the time, Pallas kernels for 0%

commit v1 on v0

--- a/solution.py
+++ b/solution.py
@@ -106,7 +106,24 @@
     deviation = (aligned - mean_now[None]).astype(jnp.bfloat16)
     column_atoms = frames.shape[2]
     row_count = column_atoms * lax.axis_size("atoms") // lax.axis_size(FRAMES)
-    own_rows = lax.all_gather(deviation, "atoms", axis=2, tiled=True)
+    ways, here, step = (lax.axis_size("atoms"), lax.axis_index("atoms"), deviation.shape[2])
+    shape = [n * ways if d == 2 else n for d, n in enumerate(deviation.shape)]
+    own_rows = lax.dynamic_update_slice_in_dim(
+        jnp.zeros(shape, deviation.dtype), deviation, here * step, axis=2
+    )
+    going_up = going_down = deviation
+    for far in range(1, ways // 2 + 1):
+        going_up = lax.ppermute(going_up, "atoms", [(d, (d + 1) % ways) for d in range(ways)])
+        own_rows = lax.dynamic_update_slice_in_dim(
+            own_rows, going_up, (here - far) % ways * step, axis=2
+        )
+        if 2 * far < ways:
+            going_down = lax.ppermute(
+                going_down, "atoms", [(d, (d - 1) % ways) for d in range(ways)]
+            )
+            own_rows = lax.dynamic_update_slice_in_dim(
+                own_rows, going_down, (here + far) % ways * step, axis=2
+            )
     row_panel = core_and_chips(own_rows, (("frames_0", "frames_1"), "frames_2"), (1, 0), 2, 0)
     row_flat = row_panel.reshape(row_panel.shape[0], 3 * row_count)
     piece = lax.all_gather(deviation, FRAMES, axis=0, tiled=True)

time: 282 us -> 270 us (0.957)
  the two profiles are of different devices: /device:TPU:2 before, /device:TPU:1 now
where the time goes in v1:
time: 270 us; the launch traced here: 269 us
  blocking collectives  116 us (43%)
  starting transfers between devices  54.4 us (20%)
  local copies, waits for them, and re-layouts  40.1 us (15%)
  waiting for transfers between devices  26.6 us (10%)
  between operations  15.3 us (6%)
  matrix products  11.8 us (4%)
  other arithmetic  5.13 us (2%)
    all_to_all x3, blocking collectives, copy_for_each(): return lax.all_to_all(copies, axis, split_axis=0, concat_axis=0, tiled=True)  58.5 us
    all_to_all x2, blocking collectives, exchange_in_order(): lax.all_to_all(blocks, axes[k], split_axis=k, concat_axis=k, tiled=True)  57.2 us
    ppermute x7, starting transfers between devices, body(): lax.ppermute(going_down, 'atoms', [(d, (d - 1) % ways) for d in range(way...  33.3 us
    ppermute x8, starting transfers between devices, body(): lax.ppermute(going_up, 'atoms', [(d, (d + 1) % ways) for d in range(ways)])  15.7 us
    ppermute x8, waiting for transfers between devices, body(): lax.ppermute(going_up, 'atoms', [(d, (d + 1) % ways) for d in range(ways)])  12.1 us
    all_to_all x1, waiting for transfers between devices, copy_for_each(): return lax.all_to_all(copies, axis, split_axis=0, concat_axis=0, tiled=True)  8.32 us
    another operation x1, local copies, waits for them, and re-layouts, body(): row_flat = row_panel.reshape(row_panel.shape[0], 3 * row_count)  8.03 us
    dot_general x1, matrix products, contract_frames(): lax.dot_general(left_rows, right_rows, (((0,), (0,)), ((), ())), preferre...  7.42 us
  transfers between devices with their start and end apart: 17, of which 9 were waited for; matrix products, arithmetic and copies ran while one was open for 9% of the time, Pallas kernels for 0%

profile of v1, /device:TPU:1, one launch (start us, length us, event | category | flops | bytes accessed | tf_op | source)
XLA Modules:
  0.0 269.0 jit_solution(2425342773651873030)
XLA Ops:
  7.2 0.9 reduce_sum.99
  8.0 1.1 reduce_sum.98
  9.1 1.4 convolution_bitcast_fusion.2
  11.0 27.2 %all_to_all.32 = f32[16,1,771]{2,1,0:T(1,128)S(1)} all-to-all(f32[16,1,771]{2,1,0:T(1,128)S(1)} %broadcast_in_dim.11), channel_id=1, replica_groups=mesh['frames_0'=4,'frames_1'=4,'frames_2'=2,'atoms'=16] {'atoms'}, dimensions={0} | all-to-all | bytes 98688 | tf_op jit(solution)/shard_map/all_to_all | solution.py:15
  40.2 1.3 convolution_bitcast_fusion.1
  41.5 17.2 %all_to_all.33 = f32[32,3,384]{2,1,0:T(4,128)S(1)} all-to-all(f32[32,3,384]{2,1,0:T(4,128)S(1)} %broadcast_in_dim.12), channel_id=1, replica_groups=mesh['frames_0'=4,'frames_1'=4,'frames_2'=2,'atoms'=16] {'frames_0','fra..., dimensions={0} | all-to-all | bytes 294912 | tf_op jit(solution)/shard_map/all_to_all | solution.py:15
  58.9 0.5 convolution_bitcast_fusion
  59.6 14.2 %all_to_all.34 = f32[16,1,771]{2,1,0:T(1,128)S(1)} all-to-all(f32[16,1,771]{2,1,0:T(1,128)S(1)} %broadcast_in_dim.13), channel_id=1, replica_groups=mesh['frames_0'=4,'frames_1'=4,'frames_2'=2,'atoms'=16] {'atoms'}, dimensions={0} | all-to-all | bytes 98688 | tf_op jit(solution)/shard_map/all_to_all | solution.py:15
  76.1 1.1 fusion.33
  77.2 0.7 broadcast_in_dim.14
  77.9 5.4 %all-to-all-start.3 = ((f32[32,3,384]{2,1,0:T(4,128)}), f32[32,3,384]{2,1,0:T(4,128)S(1)}, u32[]{:S(2)}, u32[]{:S(2)}) async-start(f32[32,3,384]{2,1,0:T(4,128)} %broadcast_in_dim.14), calls=%async_computation.3 | async-start | bytes 393216 | tf_op jit(solution)/shard_map/all_to_all | solution.py:15
  83.4 8.3 %all-to-all-done.3 = f32[32,3,384]{2,1,0:T(4,128)S(1)} async-done(((f32[32,3,384]{2,1,0:T(4,128)}), f32[32,3,384]{2,1,0:T(4,128)S(1)}, u32[]{:S(2)}, u32[]{:S(2)}) %all-to-all-start.3) | async-done | bytes 147488 | tf_op jit(solution)/shard_map/all_to_all | solution.py:15
  92.1 0.7 constant_dynamic-update-slice_fusion
  92.8 3.0 %collective-permute-start.1 = (bf16[64,3,384]{2,1,0:T(4,128)(2,1)S(1)}, bf16[64,3,384]{2,1,0:T(4,128)(2,1)S(1)}, u32[]{:S(2)}, u32[]{:S(2)}) collective-permute-start(bf16[64,3,384]{2,1,0:T(4,128)(2,1)S(1)} %subtract_convert_fusion), channel_id=1, source_target_pairs={{0,15},{1,0},{2,1},{3,2},{4,3},{5,4},{6,5},{7,6},{8,7},{9,8},{10,9... | collective-permute-start | bytes 442376 | tf_op jit(solution)/shard_map/ppermute | solution.py:121
  95.8 2.3 collective-permute-start
  98.4 2.7 collective-permute-done.1
  101.1 4.2 %collective-permute-start.3 = (bf16[64,3,384]{2,1,0:T(4,128)(2,1)S(1)}, bf16[64,3,384]{2,1,0:T(4,128)(2,1)S(1)}, u32[]{:S(2)}, u32[]{:S(2)}) collective-permute-start(bf16[64,3,384]{2,1,0:T(4,128)(2,1)S(1)} %collective-permute-done.1), channel_id=1, source_target_pairs={{0,15},{1,0},{2,1},{3,2},{4,3},{5,4},{6,5},{7,6},{8,7},{9,8},{10,9... | collective-permute-start | bytes 442376 | tf_op jit(solution)/shard_map/ppermute | solution.py:121
  105.3 1.9 collective-permute-start.2
  107.3 1.2 collective-permute-done.3
  108.5 5.3 %collective-permute-start.5 = (bf16[64,3,384]{2,1,0:T(4,128)(2,1)S(1)}, bf16[64,3,384]{2,1,0:T(4,128)(2,1)S(1)}, u32[]{:S(2)}, u32[]{:S(2)}) collective-permute-start(bf16[64,3,384]{2,1,0:T(4,128)(2,1)S(1)} %collective-permute-done.3), channel_id=1, source_target_pairs={{0,15},{1,0},{2,1},{3,2},{4,3},{5,4},{6,5},{7,6},{8,7},{9,8},{10,9... | collective-permute-start | bytes 442376 | tf_op jit(solution)/shard_map/ppermute | solution.py:121
  113.8 1.9 collective-permute-start.4
  115.9 0.6 collective-permute-done.5
  116.4 5.0 %collective-permute-start.7 = (bf16[64,3,384]{2,1,0:T(4,128)(2,1)S(1)}, bf16[64,3,384]{2,1,0:T(4,128)(2,1)S(1)}, u32[]{:S(2)}, u32[]{:S(2)}) collective-permute-start(bf16[64,3,384]{2,1,0:T(4,128)(2,1)S(1)} %collective-permute-done.5), channel_id=1, source_target_pairs={{0,15},{1,0},{2,1},{3,2},{4,3},{5,4},{6,5},{7,6},{8,7},{9,8},{10,9... | collective-permute-start | bytes 442376 | tf_op jit(solution)/shard_map/ppermute | solution.py:121
  121.5 1.9 collective-permute-start.6
  123.5 0.6 collective-permute-done.7
  124.0 5.0 %collective-permute-start.9 = (bf16[64,3,384]{2,1,0:T(4,128)(2,1)S(1)}, bf16[64,3,384]{2,1,0:T(4,128)(2,1)S(1)}, u32[]{:S(2)}, u32[]{:S(2)}) collective-permute-start(bf16[64,3,384]{2,1,0:T(4,128)(2,1)S(1)} %collective-permute-done.7), channel_id=1, source_target_pairs={{0,15},{1,0},{2,1},{3,2},{4,3},{5,4},{6,5},{7,6},{8,7},{9,8},{10,9... | collective-permute-start | bytes 442376 | tf_op jit(solution)/shard_map/ppermute | solution.py:121
  129.1 1.9 collective-permute-start.8
  131.1 0.6 collective-permute-done.9
  131.7 5.4 %collective-permute-start.11 = (bf16[64,3,384]{2,1,0:T(4,128)(2,1)S(1)}, bf16[64,3,384]{2,1,0:T(4,128)(2,1)S(1)}, u32[]{:S(2)}, u32[]{:S(2)}) collective-permute-start(bf16[64,3,384]{2,1,0:T(4,128)(2,1)S(1)} %collective-permute-done.9), channel_id=1, source_target_pairs={{0,15},{1,0},{2,1},{3,2},{4,3},{5,4},{6,5},{7,6},{8,7},{9,8},{10,9... | collective-permute-start | bytes 442376 | tf_op jit(solution)/shard_map/ppermute | solution.py:121
  137.1 1.9 collective-permute-start.10
  139.1 0.6 collective-permute-done.11
  139.7 5.4 %collective-permute-start.13 = (bf16[64,3,384]{2,1,0:T(4,128)(2,1)S(1)}, bf16[64,3,384]{2,1,0:T(4,128)(2,1)S(1)}, u32[]{:S(2)}, u32[]{:S(2)}) collective-permute-start(bf16[64,3,384]{2,1,0:T(4,128)(2,1)S(1)} %collective-permute-done.11), channel_id=1, source_target_pairs={{0,15},{1,0},{2,1},{3,2},{4,3},{5,4},{6,5},{7,6},{8,7},{9,8},{10,9... | collective-permute-start | bytes 442376 | tf_op jit(solution)/shard_map/ppermute | solution.py:121
  145.1 1.9 collective-permute-start.12
  147.1 5.6 %collective-permute-done.12 = bf16[64,3,384]{2,1,0:T(4,128)(2,1)S(1)} collective-permute-done((bf16[64,3,384]{2,1,0:T(4,128)(2,1)S(1)}, bf16[64,3,384]{2,1,0:T(4,128)(2,1)S(1)}, u32[]{:S(2)}, u32[]{:S(2)}) %collective-permute-start.12) | collective-permute-done | bytes 147488 | tf_op jit(solution)/shard_map/ppermute | solution.py:116
  152.7 1.9 collective-permute-start.14
  154.7 6.4 %collective-permute-done.14 = bf16[64,3,384]{2,1,0:T(4,128)(2,1)S(1)} collective-permute-done((bf16[64,3,384]{2,1,0:T(4,128)(2,1)S(1)}, bf16[64,3,384]{2,1,0:T(4,128)(2,1)S(1)}, u32[]{:S(2)}, u32[]{:S(2)}) %collective-permute-start.14) | collective-permute-done | bytes 147488 | tf_op jit(solution)/shard_map/ppermute | solution.py:116
  161.2 4.5 %reshape.5858 = bf16[64,3,32,192]{3,2,0,1:T(8,128)(2,1)} reshape(bf16[64,3,6144]{2,0,1:T(8,128)(2,1)S(1)} %copy_dynamic-update-slice_fusion) | data formatting | bytes 4718592 | tf_op jit(solution)/shard_map/reshape | solution.py:34
  165.8 4.3 %reshape.5859 = bf16[16,2,64,3,192]{4,1,0,2,3:T(2,128)(2,1)S(1)} reshape(bf16[32,64,3,192]{3,0,1,2:T(8,128)(2,1)} %bitcast.395) | data formatting | bytes 4718592 | tf_op jit(solution)/shard_map/reshape | solution.py:46
  170.1 1.8 copy.117
  171.8 14.0 %all_to_all.35 = bf16[16,2,64,3,192]{4,2,3,0,1:T(8,128)(2,1)S(1)} all-to-all(bf16[16,2,64,3,192]{4,2,3,0,1:T(8,128)(2,1)S(1)} %copy.117), channel_id=1, replica_groups=mesh['frames_0'=4,'frames_1'=4,'frames_2'=2,'atoms'=16] {'frames_2'}, dimensions={1} | all-to-all | bytes 4718592 | tf_op jit(solution)/shard_map/all_to_all | solution.py:48
  185.9 0.4 copy.118
  186.3 43.1 %all_to_all.36 = bf16[16,2,64,3,192]{4,2,3,1,0:T(8,128)(2,1)S(1)} all-to-all(bf16[16,2,64,3,192]{4,2,3,1,0:T(8,128)(2,1)S(1)} %copy.118), channel_id=1, replica_groups=mesh['frames_0'=4,'frames_1'=4,'frames_2'=2,'atoms'=16] {'frames_0','fra..., dimensions={0} | all-to-all | bytes 4718592 | tf_op jit(solution)/shard_map/all_to_all | solution.py:48
  229.4 5.0 %copy.119 = bf16[16,2,64,3,192]{4,3,2,1,0:T(4,128)(2,1)} copy(bf16[16,2,64,3,192]{4,2,3,1,0:T(8,128)(2,1)S(1)} %all_to_all.36) | data formatting | bytes 4718592 | tf_op jit(solution)/shard_map/all_to_all | solution.py:48
  234.4 8.0 %reshape_reshape_reshape.3 = bf16[2048,576]{1,0:T(8,128)(2,1)S(1)} reshape(bf16[16,2,64,3,192]{4,3,2,1,0:T(4,128)(2,1)} %copy.119) | data formatting | bytes 4718592 | tf_op jit(solution)/shard_map/reshape;reshape;reshape | solution.py:128
  242.5 6.7 %copy.121 = bf16[2048,3,384]{0,2,1:T(8,128)(2,1)} copy(bf16[2048,3,384]{2,0,1:T(8,128)(2,1)} %all-gather.2.cloned.1.call-done) | data formatting | bytes 9437184 | tf_op jit(solution)/shard_map/all_gather | solution.py:129
  249.2 7.4 %convolution_multiply_fusion = f32[576,1152]{1,0:T(8,128)} fusion(bf16[2048,576]{1,0:T(8,128)(2,1)S(1)} %reshape_reshape_reshape.3, bf16[2048,1152]{0,1:T(8,128)(2,1)} %bitcast.396), kind=kOutput, calls=%fused_computation | convolution fusion | flops 2718572544 | bytes 9732096 | tf_op jit(solution)/shard_map/dot_general | solution.py:82
  256.7 3.7 %reshape.5861 = f32[3,192,3,384]{3,2,1,0:T(4,128)S(1)} reshape(f32[576,1152]{1,0:T(8,128)} %convolution_multiply_fusion) | data formatting | bytes 5308416 | tf_op jit(solution)/shard_map/reshape | solution.py:131
  260.4 1.7 copy.122
  (162 shorter events, 5.8 us)
Async XLA Ops:
  7.2 51.7 %copy-start = (f32[64,3,384]{2,0,1:T(8,128)S(1)}, f32[64,3,384]{2,0,1:T(8,128)}, u32[]{:S(2)}) copy-start(f32[64,3,384]{2,0,1:T(8,128)} %param.2) | copy-start | bytes 884740
  77.9 13.8 %all-to-all-start.3 = ((f32[32,3,384]{2,1,0:T(4,128)}), f32[32,3,384]{2,1,0:T(4,128)S(1)}, u32[]{:S(2)}, u32[]{:S(2)}) async-start(f32[32,3,384]{2,1,0:T(4,128)} %broadcast_in_dim.14), calls=%async_computation.3 | async-start | bytes 393216 | tf_op jit(solution)/shard_map/all_to_all | solution.py:15
  83.3 159.2 %all-gather.2.cloned.1.call-start = ((), (), s32[]{:S(2)}) async-start(), calls=%async_computation.6 | async-start | bytes 4866048 | tf_op jit(solution)/shard_map/all_gather | solution.py:129
  91.8 15.5 %copy-start.1 = (f32[3,384]{1,0:T(4,128)}, f32[3,384]{1,0:T(4,128)S(1)}, u32[]{:S(2)}) copy-start(f32[3,384]{1,0:T(4,128)S(1)} %broadcast_multiply_fusion) | copy-start | bytes 13828
  92.8 8.2 %collective-permute-start.1 = (bf16[64,3,384]{2,1,0:T(4,128)(2,1)S(1)}, bf16[64,3,384]{2,1,0:T(4,128)(2,1)S(1)}, u32[]{:S(2)}, u32[]{:S(2)}) collective-permute-start(bf16[64,3,384]{2,1,0:T(4,128)(2,1)S(1)} %subtract_convert_fusion), channel_id=1, source_target_pairs={{0,15},{1,0},{2,1},{3,2},{4,3},{5,4},{6,5},{7,6},{8,7},{9,8},{10,9... | collective-permute-start | bytes 442376 | tf_op jit(solution)/shard_map/ppermute | solution.py:121
  95.8 9.4 %collective-permute-start = (bf16[64,3,384]{2,1,0:T(4,128)(2,1)S(1)}, bf16[64,3,384]{2,1,0:T(4,128)(2,1)S(1)}, u32[]{:S(2)}, u32[]{:S(2)}) collective-permute-start(bf16[64,3,384]{2,1,0:T(4,128)(2,1)S(1)} %subtract_convert_fusion), channel_id=1, source_target_pairs={{0,1},{1,2},{2,3},{3,4},{4,5},{5,6},{6,7},{7,8},{8,9},{9,10},{10,1... | collective-permute-start | bytes 442376 | tf_op jit(solution)/shard_map/ppermute | solution.py:116
  101.1 7.4 %collective-permute-start.3 = (bf16[64,3,384]{2,1,0:T(4,128)(2,1)S(1)}, bf16[64,3,384]{2,1,0:T(4,128)(2,1)S(1)}, u32[]{:S(2)}, u32[]{:S(2)}) collective-permute-start(bf16[64,3,384]{2,1,0:T(4,128)(2,1)S(1)} %collective-permute-done.1), channel_id=1, source_target_pairs={{0,15},{1,0},{2,1},{3,2},{4,3},{5,4},{6,5},{7,6},{8,7},{9,8},{10,9... | collective-permute-start | bytes 442376 | tf_op jit(solution)/shard_map/ppermute | solution.py:121
  105.3 8.6 %collective-permute-start.2 = (bf16[64,3,384]{2,1,0:T(4,128)(2,1)S(1)}, bf16[64,3,384]{2,1,0:T(4,128)(2,1)S(1)}, u32[]{:S(2)}, u32[]{:S(2)}) collective-permute-start(bf16[64,3,384]{2,1,0:T(4,128)(2,1)S(1)} %collective-permute-done), channel_id=1, source_target_pairs={{0,1},{1,2},{2,3},{3,4},{4,5},{5,6},{6,7},{7,8},{8,9},{9,10},{10,1... | collective-permute-start | bytes 442376 | tf_op jit(solution)/shard_map/ppermute | solution.py:116
  108.5 7.9 %collective-permute-start.5 = (bf16[64,3,384]{2,1,0:T(4,128)(2,1)S(1)}, bf16[64,3,384]{2,1,0:T(4,128)(2,1)S(1)}, u32[]{:S(2)}, u32[]{:S(2)}) collective-permute-start(bf16[64,3,384]{2,1,0:T(4,128)(2,1)S(1)} %collective-permute-done.3), channel_id=1, source_target_pairs={{0,15},{1,0},{2,1},{3,2},{4,3},{5,4},{6,5},{7,6},{8,7},{9,8},{10,9... | collective-permute-start | bytes 442376 | tf_op jit(solution)/shard_map/ppermute | solution.py:121
  113.8 7.6 %collective-permute-start.4 = (bf16[64,3,384]{2,1,0:T(4,128)(2,1)S(1)}, bf16[64,3,384]{2,1,0:T(4,128)(2,1)S(1)}, u32[]{:S(2)}, u32[]{:S(2)}) collective-permute-start(bf16[64,3,384]{2,1,0:T(4,128)(2,1)S(1)} %collective-permute-done.2), channel_id=1, source_target_pairs={{0,1},{1,2},{2,3},{3,4},{4,5},{5,6},{6,7},{7,8},{8,9},{9,10},{10,1... | collective-permute-start | bytes 442376 | tf_op jit(solution)/shard_map/ppermute | solution.py:116
  116.4 7.6 %collective-permute-start.7 = (bf16[64,3,384]{2,1,0:T(4,128)(2,1)S(1)}, bf16[64,3,384]{2,1,0:T(4,128)(2,1)S(1)}, u32[]{:S(2)}, u32[]{:S(2)}) collective-permute-start(bf16[64,3,384]{2,1,0:T(4,128)(2,1)S(1)} %collective-permute-done.5), channel_id=1, source_target_pairs={{0,15},{1,0},{2,1},{3,2},{4,3},{5,4},{6,5},{7,6},{8,7},{9,8},{10,9... | collective-permute-start | bytes 442376 | tf_op jit(solution)/shard_map/ppermute | solution.py:121
  121.5 7.6 %collective-permute-start.6 = (bf16[64,3,384]{2,1,0:T(4,128)(2,1)S(1)}, bf16[64,3,384]{2,1,0:T(4,128)(2,1)S(1)}, u32[]{:S(2)}, u32[]{:S(2)}) collective-permute-start(bf16[64,3,384]{2,1,0:T(4,128)(2,1)S(1)} %collective-permute-done.4), channel_id=1, source_target_pairs={{0,1},{1,2},{2,3},{3,4},{4,5},{5,6},{6,7},{7,8},{8,9},{9,10},{10,1... | collective-permute-start | bytes 442376 | tf_op jit(solution)/shard_map/ppermute | solution.py:116
  124.0 7.6 %collective-permute-start.9 = (bf16[64,3,384]{2,1,0:T(4,128)(2,1)S(1)}, bf16[64,3,384]{2,1,0:T(4,128)(2,1)S(1)}, u32[]{:S(2)}, u32[]{:S(2)}) collective-permute-start(bf16[64,3,384]{2,1,0:T(4,128)(2,1)S(1)} %collective-permute-done.7), channel_id=1, source_target_pairs={{0,15},{1,0},{2,1},{3,2},{4,3},{5,4},{6,5},{7,6},{8,7},{9,8},{10,9... | collective-permute-start | bytes 442376 | tf_op jit(solution)/shard_map/ppermute | solution.py:121
  129.1 8.0 %collective-permute-start.8 = (bf16[64,3,384]{2,1,0:T(4,128)(2,1)S(1)}, bf16[64,3,384]{2,1,0:T(4,128)(2,1)S(1)}, u32[]{:S(2)}, u32[]{:S(2)}) collective-permute-start(bf16[64,3,384]{2,1,0:T(4,128)(2,1)S(1)} %collective-permute-done.6), channel_id=1, source_target_pairs={{0,1},{1,2},{2,3},{3,4},{4,5},{5,6},{6,7},{7,8},{8,9},{9,10},{10,1... | collective-permute-start | bytes 442376 | tf_op jit(solution)/shard_map/ppermute | solution.py:116
  131.7 8.0 %collective-permute-start.11 = (bf16[64,3,384]{2,1,0:T(4,128)(2,1)S(1)}, bf16[64,3,384]{2,1,0:T(4,128)(2,1)S(1)}, u32[]{:S(2)}, u32[]{:S(2)}) collective-permute-start(bf16[64,3,384]{2,1,0:T(4,128)(2,1)S(1)} %collective-permute-done.9), channel_id=1, source_target_pairs={{0,15},{1,0},{2,1},{3,2},{4,3},{5,4},{6,5},{7,6},{8,7},{9,8},{10,9... | collective-permute-start | bytes 442376 | tf_op jit(solution)/shard_map/ppermute | solution.py:121
  137.1 8.0 %collective-permute-start.10 = (bf16[64,3,384]{2,1,0:T(4,128)(2,1)S(1)}, bf16[64,3,384]{2,1,0:T(4,128)(2,1)S(1)}, u32[]{:S(2)}, u32[]{:S(2)}) collective-permute-start(bf16[64,3,384]{2,1,0:T(4,128)(2,1)S(1)} %collective-permute-done.8), channel_id=1, source_target_pairs={{0,1},{1,2},{2,3},{3,4},{4,5},{5,6},{6,7},{7,8},{8,9},{9,10},{10,1... | collective-permute-start | bytes 442376 | tf_op jit(solution)/shard_map/ppermute | solution.py:116
  139.7 15.0 %collective-permute-start.13 = (bf16[64,3,384]{2,1,0:T(4,128)(2,1)S(1)}, bf16[64,3,384]{2,1,0:T(4,128)(2,1)S(1)}, u32[]{:S(2)}, u32[]{:S(2)}) collective-permute-start(bf16[64,3,384]{2,1,0:T(4,128)(2,1)S(1)} %collective-permute-done.11), channel_id=1, source_target_pairs={{0,15},{1,0},{2,1},{3,2},{4,3},{5,4},{6,5},{7,6},{8,7},{9,8},{10,9... | collective-permute-start | bytes 442376 | tf_op jit(solution)/shard_map/ppermute | solution.py:121
  145.1 7.6 %collective-permute-start.12 = (bf16[64,3,384]{2,1,0:T(4,128)(2,1)S(1)}, bf16[64,3,384]{2,1,0:T(4,128)(2,1)S(1)}, u32[]{:S(2)}, u32[]{:S(2)}) collective-permute-start(bf16[64,3,384]{2,1,0:T(4,128)(2,1)S(1)} %collective-permute-done.10), channel_id=1, source_target_pairs={{0,1},{1,2},{2,3},{3,4},{4,5},{5,6},{6,7},{7,8},{8,9},{9,10},{10,1... | collective-permute-start | bytes 442376 | tf_op jit(solution)/shard_map/ppermute | solution.py:116
  152.7 8.5 %collective-permute-start.14 = (bf16[64,3,384]{2,1,0:T(4,128)(2,1)S(1)}, bf16[64,3,384]{2,1,0:T(4,128)(2,1)S(1)}, u32[]{:S(2)}, u32[]{:S(2)}) collective-permute-start(bf16[64,3,384]{2,1,0:T(4,128)(2,1)S(1)} %collective-permute-done.12), channel_id=1, source_target_pairs={{0,1},{1,2},{2,3},{3,4},{4,5},{5,6},{6,7},{7,8},{8,9},{9,10},{10,1... | collective-permute-start | bytes 442376 | tf_op jit(solution)/shard_map/ppermute | solution.py:116
Sparse Core Ops, SparseCore 0:
  93.0 50.6 all-gather.1
